TPU v7x, 32 devices: a whole 2x2x4 slice. The times are simulated.
32 devices in a mesh: cluster: 8 (over z, x), camera: 4 (over y, core).
Axes of the slice: x: 2, y: 2, z: 4, core: 2. Of those that a mesh axis runs over, the one named last changes fastest.
Arguments:
- counts: int32 [8], replicated, may hold values from 1 to 16, as said below
- tiles: int32 [128, 4], replicated, may hold values from 0 to 3
- cam_jac: float32 [128, 128, 512], P('cluster', None, 'camera'), may hold values from -0.6 to 0.6
- point_jac: float32 [128, 128, 3, 512], P('cluster', None, None, 'camera'), may hold values from -0.15625 to 0.15625
- point_inv: float32 [128, 3, 3, 512], P('cluster', None, None, 'camera'), may hold values from -1 to 1, as said below
Outputs:
- reduced: float32 [4, 512, 2048], P('camera', 'cluster')
Inputs may be any that keep to these rules, and one draw needn't show every extreme that they name: For every device i below 4, exactly one of the devices i and i + 4 holds 13 to 16 live clusters and the other 1 to 8; at least 4 devices hold exactly 16. The live clusters of a device are its first counts slots. Every 3x3 block point_inv[c, :, :, p] is symmetric and positive definite.
All inputs are finite; a program needn't handle non-finite values.
Results may differ from a plain program's by a relative error of at most 0.0003.
Values sent between devices are 32-bit elements; how exact they have to be, the bound alone decides.
A program may use at most 64 MiB of HBM per device.

v0:
```python
import jax
import jax.numpy as jnp
from jax import lax
from jax.sharding import PartitionSpec as P

KEEP = 12
EXTRA = 4
GT = 4


HIGHEST_PRECISION = lax.Precision.HIGHEST


def passed_along(block, axis, distance):
    devices = range(lax.axis_size(axis))
    route = [((i - distance) % len(devices), i) for i in devices]
    return lax.ppermute(block, axis, route)


def contract_rows(left, right):
    return lax.dot_general(
        left,
        right,
        (((0,), (0,)), ((), ())),
        precision=HIGHEST_PRECISION,
        preferred_element_type=jnp.float32,
    )


def on_device(counts, tiles, cam_jac, point_jac, point_inv):
    device = lax.axis_index("cluster")
    camera = lax.axis_index("camera")
    devices = lax.axis_size("cluster")
    cameras = lax.axis_size("camera")
    slot_count = cam_jac.shape[0]
    tile_width = cam_jac.shape[2]
    slot_ids = jnp.arange(slot_count, dtype=jnp.int32)
    local_live = slot_ids < counts[device]
    local_ids = device * slot_count + slot_ids
    half_count = devices // 2
    partner = (device + half_count) % devices
    device_over = counts[device] > KEEP
    offsets = jnp.arange(EXTRA, dtype=jnp.int32)
    arrived = passed_along(
        (cam_jac[KEEP:], point_jac[KEEP:], point_inv[KEEP:]), "cluster", half_count
    )
    helper_live = jnp.logical_not(device_over) & (offsets < counts[partner] - KEEP)
    kept_local = KEEP - EXTRA

    def choose_rows(local_rows, remote_rows):
        return jnp.where(
            device_over,
            local_rows[:KEEP],
            jnp.concatenate([local_rows[:kept_local], remote_rows], axis=0),
        )

    item_jac = choose_rows(cam_jac, arrived[0])
    item_points = choose_rows(point_jac, arrived[1])
    item_inv = choose_rows(point_inv, arrived[2])
    item_live = choose_rows(local_live, helper_live)
    item_ids = choose_rows(local_ids, partner * slot_count + KEEP + offsets)
    masked = item_jac * item_live.astype(jnp.float32)[:, None, None]
    full_jac = lax.all_gather(masked, "camera", axis=2, tiled=True)
    item_count = masked.shape[0]
    row_count = masked.shape[1]
    flat_points = item_points.reshape(item_count, row_count, -1)
    item_tiles = tiles[item_ids]
    group_width = GT * tile_width
    accumulator = jnp.zeros((group_width, group_width * cameras), jnp.float32)
    weighted = jnp.einsum("nrjp,njkp->nrkp", item_points, item_inv, precision=HIGHEST_PRECISION)
    coupled_local = lax.dot_general(
        weighted.reshape(item_count, row_count, -1),
        flat_points,
        (((2,), (2,)), ((0,), (0,))),
        precision=HIGHEST_PRECISION,
        preferred_element_type=jnp.float32,
    )
    coupled = lax.psum(coupled_local, "camera")

    def schur_rows(item_index):
        full_panel = full_jac[item_index]
        reduced_panel = full_panel - jnp.dot(
            coupled[item_index],
            full_panel,
            precision=HIGHEST_PRECISION,
            preferred_element_type=jnp.float32,
        )
        return contract_rows(masked[item_index], reduced_panel)

    def accumulate(item_index, accumulator):
        rows_block = schur_rows(item_index)
        row_start = item_tiles[item_index, camera] * tile_width
        for group_index in range(cameras):
            col_start = (group_index * GT + item_tiles[item_index, group_index]) * tile_width
            current = lax.dynamic_slice(
                accumulator, (row_start, col_start), (tile_width, tile_width)
            )
            updated = (
                current + rows_block[:, group_index * tile_width : (group_index + 1) * tile_width]
            )
            accumulator = lax.dynamic_update_slice(accumulator, updated, (row_start, col_start))
        return accumulator

    accumulator = lax.fori_loop(0, item_count, accumulate, accumulator)
    summed = lax.psum_scatter(accumulator, "cluster", scatter_dimension=0, tiled=True)
    return summed[None]


def solution(mesh):
    in_specs = (
        P(),
        P(),
        P("cluster", None, "camera"),
        P("cluster", None, None, "camera"),
        P("cluster", None, None, "camera"),
    )
    out_specs = P("camera", "cluster", None)
    return jax.shard_map(
        on_device, mesh=mesh, in_specs=in_specs, out_specs=out_specs, check_vma=False
    )
```

profile of v0, /device:TPU:0, one launch (start us, length us, event | category | flops | bytes accessed | tf_op | source)
XLA Modules:
  0.0 393.7 jit_solution(15243090770504865096)
XLA Ops:
  6.5 2.2 slice.87
  8.8 2.3 copy.24
  11.1 4.0 %collective-permute-start.2 = (f32[4,128,3,128]{1,3,2,0:T(8,128)}, f32[4,128,3,128]{1,3,2,0:T(8,128)}, u32[]{:S(2)}, u32[]{:S(2)}) collective-permute-start(f32[4,128,3,128]{1,3,2,0:T(8,128)} %copy.24), channel_id=1, source_target_pairs={{16,0},{20,4},{24,8},{28,12},{0,16},{4,20},{8,24},{12,28},{17,1},{... | collective-permute-start | bytes 2359304 | tf_op jit(solution)/shard_map/ppermute | solution.py:17
  15.9 1.7 slice.79
  17.5 2.9 collective-permute-start
  24.8 3.1 copy.23
  27.9 2.0 copy.22
  29.8 27.1 %collective-permute-done.1 = f32[4,3,3,128]{3,0,2,1:T(4,128)S(1)} collective-permute-done((f32[4,3,3,128]{3,0,2,1:T(4,128)S(1)}, f32[4,3,3,128]{3,0,2,1:T(4,128)S(1)}, u32[]{:S(2)}, u32[]{:S(2)}) %collective-permute-start.1) | collective-permute-done | bytes 18464 | tf_op jit(solution)/shard_map/ppermute | solution.py:17
  56.9 2.0 copy.14
  59.0 2.8 maximum_select_fusion
  61.8 11.4 %fusion.15 = f32[12,128,3,128]{1,2,3,0:T(4,128)S(1)} fusion(f32[12,3,3,128]{1,2,3,0:T(4,128)S(1)} %copy.14, f32[12,128,3,128]{1,3,2,0:T(8,128)S(1)} %maximum_select_fusion), kind=kOutput, calls=%fused_computation.26 | convolution fusion | flops 21233664 | bytes 4773888 | tf_op jit(solution)/shard_map/nrjp,njkp->nrkp/dot_general | solution.py:70
  73.5 5.0 %fusion.21 = f32[12,128,128]{2,1,0:T(8,128)} fusion(f32[12,128,384]{1,2,0:T(8,128)S(1)} %bitcast.46, f32[12,128,384]{1,2,0:T(8,128)S(1)} %bitcast.45), kind=kOutput, calls=%fused_computation.40 | convolution fusion | flops 905969664 | bytes 5505024 | tf_op jit(solution)/shard_map/dot_general | solution.py:71
  80.7 32.4 %all-reduce.2.cloned.1.call-done = f32[12,128,128]{2,1,0:T(8,128)} async-done(((f32[12,128,128]{2,1,0:T(8,128)}), f32[12,128,128]{2,1,0:T(8,128)}) %all-reduce.2.cloned.1.call-update) | async-done | bytes 786448 | tf_op jit(solution)/shard_map/psum | solution.py:78
  113.0 30.6 %all-gather.2.cloned.1.call-done = f32[12,128,512]{2,1,0:T(8,128)} async-done(((f32[12,128,128]{2,1,0:T(8,128)}), f32[12,128,512]{2,1,0:T(8,128)}) %all-gather.2.cloned.1.call-update) | async-done | bytes 3145744 | tf_op jit(solution)/shard_map/all_gather | solution.py:63
  143.6 2.5 broadcast_in_dim.10
  146.1 152.5 %while.15 = (s32[]{:T(128)}, f32[512,2048]{1,0:T(8,128)}, s32[12,4]{0,1:T(4,128)S(1)}, s32[]{:T(128)}, f32[12,128,128]{2,1,0:T(8,128)}, /*index=5*/f32[12,128,51...) while((s32[]{:T(128)}, f32[512,2048]{1,0:T(8,128)}, ...), condition=%wide.region_2.3_spmd, body=%wide.region_1.2_spmd.sunk | while | flops 201457664 | bytes 1967603 | solution.py:104
  150.0 1.6 convolution_subtract_fusion.2
  152.8 1.5 fusion.40
  154.3 1.5 fusion.41
  155.8 1.5 fusion.42
  157.3 1.5 fusion.43
  162.7 1.5 convolution_subtract_fusion.2
  165.4 1.5 fusion.40
  166.9 1.5 fusion.41
  169.9 1.5 fusion.43
  175.3 1.5 convolution_subtract_fusion.2
  178.1 1.5 fusion.40
  179.6 1.5 fusion.41
  181.1 1.5 fusion.42
  182.6 1.5 fusion.43
  188.0 1.6 convolution_subtract_fusion.2
  190.8 1.5 fusion.40
  192.3 1.5 fusion.41
  195.3 1.5 fusion.43
  200.7 1.6 convolution_subtract_fusion.2
  203.6 1.5 fusion.40
  205.1 1.5 fusion.41
  208.0 1.5 fusion.43
  213.4 1.6 convolution_subtract_fusion.2
  216.3 1.5 fusion.40
  219.3 1.5 fusion.42
  220.8 1.5 fusion.43
  226.2 1.6 convolution_subtract_fusion.2
  229.0 1.5 fusion.40
  230.5 1.5 fusion.41
  232.0 1.5 fusion.42
  233.5 1.5 fusion.43
  238.9 1.6 convolution_subtract_fusion.2
  241.8 1.5 fusion.40
  246.3 1.5 fusion.43
  251.7 1.6 convolution_subtract_fusion.2
  254.5 1.5 fusion.40
  257.5 1.5 fusion.42
  264.4 1.5 convolution_subtract_fusion.2
  267.2 1.5 fusion.40
  268.7 1.5 fusion.41
  271.7 1.5 fusion.43
  277.1 1.6 convolution_subtract_fusion.2
  279.9 1.5 fusion.40
  289.8 1.6 convolution_subtract_fusion.2
  292.6 1.5 fusion.40
  294.1 1.5 fusion.41
  295.6 1.5 fusion.42
  298.6 88.6 %reduce-scatter.2.cloned.1.call-done = f32[64,2048]{1,0:T(8,128)} async-done(((f32[512,2048]{1,0:T(8,128)}), f32[64,2048]{1,0:T(8,128)}) %reduce-scatter.2.cloned.1.call-update) | async-done | bytes 524304 | tf_op jit(solution)/shard_map/reduce_scatter | solution.py:105
  (79 shorter events, 48.4 us)
Async XLA Ops:
  6.5 16.7 %copy-start = (f32[16,128,3,128]{3,1,2,0:T(8,128)S(1)}, f32[16,128,3,128]{3,1,2,0:T(8,128)}, u32[]{:S(2)}) copy-start(f32[16,128,3,128]{3,1,2,0:T(8,128)} %param.10) | copy-start | bytes 9437188
  6.5 13.9 %copy-start.5 = (s32[8]{0:T(128)S(1)}, s32[8]{0:T(128)}, u32[]{:S(2)}) copy-start(s32[8]{0:T(128)} %param.7) | copy-start | bytes 100
  6.5 106.5 %all-reduce.2.cloned.1.call-start = ((), (), s32[]{:S(2)}) async-start(), calls=%async_computation.2 | async-start | bytes 1572864 | tf_op jit(solution)/shard_map/psum | solution.py:78
  11.1 47.9 %collective-permute-start.2 = (f32[4,128,3,128]{1,3,2,0:T(8,128)}, f32[4,128,3,128]{1,3,2,0:T(8,128)}, u32[]{:S(2)}, u32[]{:S(2)}) collective-permute-start(f32[4,128,3,128]{1,3,2,0:T(8,128)} %copy.24), channel_id=1, source_target_pairs={{16,0},{20,4},{24,8},{28,12},{0,16},{4,20},{8,24},{12,28},{17,1},{... | collective-permute-start | bytes 2359304 | tf_op jit(solution)/shard_map/ppermute | solution.py:17
  15.9 41.1 %collective-permute-start.1 = (f32[4,3,3,128]{3,0,2,1:T(4,128)S(1)}, f32[4,3,3,128]{3,0,2,1:T(4,128)S(1)}, u32[]{:S(2)}, u32[]{:S(2)}) collective-permute-start(f32[4,3,3,128]{3,0,2,1:T(4,128)S(1)} %slice.84), channel_id=1, source_target_pairs={{16,0},{20,4},{24,8},{28,12},{0,16},{4,20},{8,24},{12,28},{17,1},{... | collective-permute-start | bytes 55304 | tf_op jit(solution)/shard_map/ppermute | solution.py:17
  17.5 61.1 %collective-permute-start = (f32[4,128,128]{2,1,0:T(8,128)}, f32[4,128,128]{2,1,0:T(8,128)S(1)}, u32[]{:S(2)}, u32[]{:S(2)}) collective-permute-start(f32[4,128,128]{2,1,0:T(8,128)} %slice.79), channel_id=1, source_target_pairs={{16,0},{20,4},{24,8},{28,12},{0,16},{4,20},{8,24},{12,28},{17,1},{... | collective-permute-start | bytes 786440 | tf_op jit(solution)/shard_map/ppermute | solution.py:17
  21.7 2.8 copy-start.1
  24.8 32.2 %copy-start.3 = (f32[16,3,3,128]{3,0,2,1:T(8,128)S(1)}, f32[16,3,3,128]{3,0,2,1:T(8,128)}, u32[]{:S(2)}) copy-start(f32[16,3,3,128]{3,0,2,1:T(8,128)} %param.11) | copy-start | bytes 221188
  24.8 32.1 %slice-start.1 = ((f32[16,3,3,128]{3,0,2,1:T(8,128)}), f32[8,3,3,128]{3,0,2,1:T(8,128)S(1)}, s32[]{:S(2)}) async-start(f32[16,3,3,128]{3,0,2,1:T(8,128)} %param.11), calls=%async_computation.5 | async-start | bytes 73728 | tf_op jit(solution)/shard_map/slice | solution.py:54
  73.4 5.2 %copy-start.2 = (f32[16,128,128]{2,1,0:T(8,128)S(1)}, f32[16,128,128]{2,1,0:T(8,128)}, u32[]{:S(2)}) copy-start(f32[16,128,128]{2,1,0:T(8,128)} %param.9) | copy-start | bytes 3145732
  73.5 5.2 %slice-start = ((f32[16,128,128]{2,1,0:T(8,128)}), f32[8,128,128]{2,1,0:T(8,128)S(1)}, s32[]{:S(2)}) async-start(f32[16,128,128]{2,1,0:T(8,128)} %param.9), calls=%async_computation.4 | async-start | bytes 1048576 | tf_op jit(solution)/shard_map/slice | solution.py:54
  78.5 1.3 copy-start.4
  78.5 65.1 %all-gather.2.cloned.1.call-start = ((), (), s32[]{:S(2)}) async-start(), calls=%async_computation.1 | async-start | bytes 3932160 | tf_op jit(solution)/shard_map/all_gather | solution.py:63
  79.7 307.5 %reduce-scatter.2.cloned.1.call-start = ((), (), s32[]{:S(2)}) async-start(), calls=%async_computation.3 | async-start | bytes 4718592 | tf_op jit(solution)/shard_map/reduce_scatter | solution.py:105
Sparse Core Ops, SparseCore 0:
  78.6 34.3 all-reduce.1
  114.6 28.9 all-gather.1
  298.7 88.4 reduce-scatter.1
where the time goes:
time: 398 us; the launch traced here: 394 us
  waiting for transfers between devices  179 us (45%)
  other arithmetic  76.1 us (19%)
  matrix products  50.4 us (13%)
  loops' own time  39.1 us (10%)
  local copies, waits for them, and re-layouts  27.6 us (7%)
  between operations  14.7 us (4%)
  starting transfers between devices  7.05 us (2%)
    reduce_scatter x1, waiting for transfers between devices, on_device(): lax.psum_scatter(accumulator, 'cluster', scatter_dimension=0, tiled=True)  88.6 us
    dynamic_update_slice x48, other arithmetic, accumulate(): lax.dynamic_update_slice(accumulator, updated, (row_start, col_start))  71.4 us
    another operation x1, loops' own time, on_device(): accumulator = lax.fori_loop(0, item_count, accumulate, accumulator)  39.1 us
    psum x1, waiting for transfers between devices, on_device(): coupled = lax.psum(coupled_local, 'camera')  32.4 us
    all_gather x1, waiting for transfers between devices, on_device(): full_jac = lax.all_gather(masked, 'camera', axis=2, tiled=True)  30.6 us
    ppermute x3, waiting for transfers between devices, passed_along(): return lax.ppermute(block, axis, route)  27.1 us
    dot_general x12, matrix products, schur_rows(): jnp.dot(coupled[item_index], full_panel, precision=HIGHEST_PRECISION, pre...  18.8 us
    dot_general x12, matrix products, contract_rows(): lax.dot_general(left, right, (((0,), (0,)), ((), ())), precision=HIGHEST_...  15.2 us
  transfers between devices with their start and end apart: 6, of which 4 were waited for; matrix products, arithmetic and copies ran while one was open for 9% of the time, Pallas kernels for 0%

commit v1 on v0

v1 whole, which is shorter than its diff:
```python
import functools
import itertools

import jax
import jax.numpy as jnp
from jax import lax
from jax.experimental import pallas as pl
from jax.experimental.pallas import tpu as pltpu
from jax.sharding import PartitionSpec as P

MESH = pl.DeviceIdType.MESH
ANY = pl.BlockSpec(memory_space=pl.ANY)
VMEM = pl.BlockSpec(memory_space=pltpu.VMEM)
SMEM = pl.BlockSpec(memory_space=pltpu.SMEM)
LANES = 128
GROUP_TILES = 4
VMEM_LIMIT = 56 * 1024 * 1024


def halves(x):
    high = x.astype(jnp.bfloat16)
    low = (x - high.astype(jnp.float32)).astype(jnp.bfloat16)
    return high, low


def dot3(left, right, dims):
    lh, ll = halves(left)
    rh, rl = halves(right)
    (ld,), (rd,) = dims
    return lax.dot_general(
        jnp.concatenate([lh, lh, ll], axis=ld),
        jnp.concatenate([rh, rl, rh], axis=rd),
        (dims, ((), ())),
        preferred_element_type=jnp.float32,
    )


def greet(peers):
    barrier = pltpu.get_barrier_semaphore()
    for peer in peers:
        pl.semaphore_signal(barrier, inc=1, device_id=peer, device_id_type=MESH)
    pl.semaphore_wait(barrier, len(peers))


def send(src, dst, send_sem, recv_sem, peer):
    return pltpu.make_async_remote_copy(
        src_ref=src, dst_ref=dst, send_sem=send_sem, recv_sem=recv_sem,
        device_id=peer, device_id_type=MESH,
    )


def exchange_kernel(
    jac, points, inv, others, coupled,
    points_here, outgoing, arrived, mine, across_in,
    send_sem, recv_sem, local_sem,
):
    camera = lax.axis_index("camera")
    core = lax.rem(camera, 2)
    sibling = {"camera": camera + 1 - 2 * core}
    across = {"camera": lax.rem(camera + 2, 4)}
    half = coupled.shape[0] // 2
    own, theirs = core * half, (1 - core) * half

    loads = [
        pltpu.make_async_copy(
            points.at[pl.ds(start, half)], points_here.at[which], local_sem.at[which]
        )
        for which, start in enumerate((theirs, own))
    ]
    for load in loads:
        load.start()
    greet([sibling, across])
    to_across = send(jac, others.at[1], send_sem.at[0], recv_sem.at[0], across)
    to_across.start()
    to_sibling = send(jac, others.at[0], send_sem.at[1], recv_sem.at[1], sibling)
    to_sibling.start()

    def couple(which, start, target):
        def body(i, carry):
            p = [points_here[which, i, :, j, :] for j in range(3)]
            w = [
                sum(p[j] * inv[start + i, j, k:k + 1, :] for j in range(3))
                for k in range(3)
            ]
            target[i] = dot3(
                jnp.concatenate(w, axis=1), jnp.concatenate(p, axis=1), (((1,), (1,)))
            )
            return carry

        loads[which].wait()
        lax.fori_loop(0, half, body, 0)

    couple(0, theirs, outgoing)
    part = send(outgoing, arrived, send_sem.at[2], recv_sem.at[2], sibling)
    part.start()
    couple(1, own, mine)
    part.wait_recv()
    mine[...] += arrived[...]
    cross = send(mine, across_in, send_sem.at[3], recv_sem.at[3], across)
    cross.start()
    to_across.wait_recv()
    forward = send(others.at[1], others.at[2], send_sem.at[4], recv_sem.at[4], sibling)
    forward.start()
    cross.wait_recv()
    block = coupled.at[pl.ds(own, half)]
    block[...] = mine[...] + across_in[...]
    back = send(block, block, send_sem.at[5], recv_sem.at[5], sibling)
    back.start()
    for copy in (to_across, to_sibling, part, cross):
        copy.wait_send()
    to_sibling.wait_recv()
    forward.wait()
    back.wait()


def exchange(jac, points, inv):
    slots, rows, width = jac.shape
    half = slots // 2
    block = pltpu.VMEM((half, rows, rows), jnp.float32)
    return pl.pallas_call(
        exchange_kernel,
        name="camera_exchange",
        out_shape=(
            jax.ShapeDtypeStruct((3, slots, rows, width), jnp.float32),
            jax.ShapeDtypeStruct((slots, rows, rows), jnp.float32),
        ),
        in_specs=[ANY, ANY, VMEM],
        out_specs=(ANY, VMEM),
        scratch_shapes=[
            pltpu.VMEM((2, half) + points.shape[1:], jnp.float32),
            block, block, block, block,
            pltpu.SemaphoreType.DMA((6,)),
            pltpu.SemaphoreType.DMA((6,)),
            pltpu.SemaphoreType.DMA((2,)),
        ],
        compiler_params=pltpu.CompilerParams(
            collective_id=0, has_side_effects=True, vmem_limit_bytes=VMEM_LIMIT
        ),
    )(jac, points, inv)


def schur_kernel(group_tiles, counts, tiles, jac, others, coupled, acc):
    camera = lax.axis_index("camera")
    device = lax.axis_index("cluster")
    slots, _, width = jac.shape
    wide = group_tiles * width
    live = counts[device]
    acc[...] = jnp.zeros_like(acc)

    def one(c):
        panel = jac[c]
        panels = [panel] + [others[r, c] for r in range(3)]
        left = panel - dot3(coupled[c], panel, (((1,), (0,))))
        left = left * jnp.where(c < live, 1.0, 0.0)
        return dot3(left, jnp.concatenate(panels, axis=1), (((0,), (0,))))

    def add(c, block):
        at = (device * slots + c) * 4
        row = pl.ds(pl.multiple_of(tiles[at + camera] * width, width), width)
        acc[row, 3 * wide:] += block[:, :width]
        for r in range(1, 4):
            tile = tiles[at + jnp.bitwise_xor(camera, r)]
            col = pl.multiple_of((r - 1) * wide + tile * width, width)
            acc[row, pl.ds(col, width)] += block[:, r * width:(r + 1) * width]

    def body(step, carry):
        blocks = [one(2 * step), one(2 * step + 1)]
        add(2 * step, blocks[0])
        add(2 * step + 1, blocks[1])
        return carry

    lax.fori_loop(0, (live + 1) // 2, body, 0)


def schur(counts, tiles, jac, others, coupled, group_tiles):
    width = jac.shape[2]
    wide = group_tiles * width
    return pl.pallas_call(
        functools.partial(schur_kernel, group_tiles),
        name="schur_sum",
        out_shape=jax.ShapeDtypeStruct((wide, 3 * wide + width), jnp.float32),
        in_specs=[SMEM, SMEM, VMEM, VMEM, VMEM],
        out_specs=VMEM,
        compiler_params=pltpu.CompilerParams(vmem_limit_bytes=VMEM_LIMIT),
    )(counts, tiles.reshape(-1), jac, others, coupled)


def parts_of(columns, bits):
    straight = tuple(range(bits))
    swapped = (1, 0) + straight[2:]
    tiles = columns // LANES
    cuts = [0, 3 * tiles // 8, 5 * tiles // 8 + 1, tiles]
    orders = [straight, swapped, straight]
    return [
        (cuts[i] * LANES, (cuts[i + 1] - cuts[i]) * LANES, orders[i]) for i in range(3)
    ]


def reduce_kernel(bits, parts, group_tiles, given, out, acc, *scratch):
    buffers, (send_sem, recv_sem, local_sem) = scratch[:-3], scratch[-3:]
    camera = lax.axis_index("camera")
    device = lax.axis_index("cluster")
    bit = [lax.rem(device // (1 << b), 2) for b in range(bits)]
    peer = [{"cluster": device + (1 - 2 * bit[b]) * (1 << b)} for b in range(bits)]
    loads = []
    for part, (first, width, _) in enumerate(parts):
        at = (slice(None),) * (bits + 1) + (pl.ds(first, width),)
        loads.append(pltpu.make_async_copy(given.at[at], acc.at[at], local_sem.at[part]))
        loads[-1].start()
    greet(peer)

    def region(part, step, flip):
        start, width, order = parts[part]
        index = [slice(None)] * bits
        for b in order[:step]:
            index[bits - 1 - b] = bit[b]
        b = order[step]
        index[bits - 1 - b] = 1 - bit[b] if flip else bit[b]
        return index, pl.ds(start, width)

    def start(part, step):
        index, columns = region(part, step, True)
        which = part * bits + step
        source = acc if step else given
        copy = send(
            source.at[tuple(index) + (slice(None), columns)], buffers[which],
            send_sem.at[which], recv_sem.at[which], peer[parts[part][2][step]],
        )
        copy.start()
        return copy

    copies = {(part, 0): start(part, 0) for part in range(len(parts))}
    for step in range(bits):
        for part in range(len(parts)):
            if step == 0:
                loads[part].wait()
            copies[part, step].wait_recv()
            index, columns = region(part, step, False)
            free = [i for i in range(bits) if isinstance(index[i], slice)]
            for place in itertools.product(range(2), repeat=len(free)):
                full = list(index)
                for i, value in zip(free, place):
                    full[i] = value
                at = tuple(full) + (slice(None), columns)
                acc[at] += buffers[part * bits + step][place]
            if step + 1 < bits:
                copies[part, step + 1] = start(part, step + 1)
    total = tuple(reversed(bit))
    rows, columns = out.shape
    wide = columns // 4
    mine = pl.multiple_of(camera * wide, wide)
    out[:, pl.ds(mine, wide)] = jnp.zeros((rows, wide), jnp.float32)
    tile = device * rows * group_tiles // wide
    width = wide // group_tiles
    out[:, pl.ds(pl.multiple_of(camera * wide + tile * width, width), width)] = acc[
        total + (slice(None), pl.ds(3 * wide, width))
    ]
    for r in range(1, 4):
        other = pl.multiple_of(jnp.bitwise_xor(camera, r) * wide, wide)
        out[:, pl.ds(other, wide)] = acc[total + (slice(None), pl.ds((r - 1) * wide, wide))]
    for copy in copies.values():
        copy.wait_send()


def reduce(acc, devices, group_tiles, cameras):
    wide, columns = acc.shape
    bits = devices.bit_length() - 1
    rows = wide // devices
    parts = parts_of(columns, bits)
    buffers = [
        pltpu.VMEM((2,) * (bits - 1 - step) + (rows, width), jnp.float32)
        for _, width, _ in parts
        for step in range(bits)
    ]
    count = len(buffers)
    return pl.pallas_call(
        functools.partial(reduce_kernel, bits, parts, group_tiles),
        name="cluster_reduce",
        out_shape=jax.ShapeDtypeStruct((rows, cameras * wide), jnp.float32),
        in_specs=[ANY],
        out_specs=VMEM,
        scratch_shapes=[pltpu.VMEM((2,) * bits + (rows, columns), jnp.float32)]
        + buffers
        + [pltpu.SemaphoreType.DMA((n,)) for n in (count, count, len(parts))],
        compiler_params=pltpu.CompilerParams(
            collective_id=1, has_side_effects=True, vmem_limit_bytes=VMEM_LIMIT
        ),
    )(acc.reshape((2,) * bits + (rows, columns)))


def on_device(counts, tiles, cam_jac, point_jac, point_inv):
    devices = lax.axis_size("cluster")
    cameras = lax.axis_size("camera")
    others, coupled = exchange(cam_jac, point_jac, point_inv)
    acc = schur(counts, tiles, cam_jac, others, coupled, GROUP_TILES)
    return reduce(acc, devices, GROUP_TILES, cameras)[None]


def solution(mesh):
    in_specs = (
        P(),
        P(),
        P("cluster", None, "camera"),
        P("cluster", None, None, "camera"),
        P("cluster", None, None, "camera"),
    )
    out_specs = P("camera", "cluster", None)
    return jax.shard_map(
        on_device,
        mesh=mesh, in_specs=in_specs, out_specs=out_specs, check_vma=False,
    )
```

time: 398 us -> 113 us (0.28); the launches traced: 394 us -> 113 us
  waiting for transfers between devices: 179 us -> 0 us
  Pallas kernels: 0 us -> 104 us
  other arithmetic: 76.1 us -> 0 us
  matrix products: 50.4 us -> 0 us
  loops' own time: 39.1 us -> 0 us
  local copies, waits for them, and re-layouts: 27.6 us -> 9.4 us
  between operations: 14.7 us -> 0.03 us
  starting transfers between devices: 7.05 us -> 0 us
    pallas_call x0 -> x3, Pallas kernels: none -> 104 us  [the longest x1 51.7 us: reduce(): pl.pallas_call(functools.partial(reduce_kernel, bits, parts, group_tiles)...]
    reduce_scatter x1 -> x0, waiting for transfers between devices: 88.6 us -> none  [on_device(): lax.psum_scatter(accumulator, 'cluster', scatter_dimension=0, tiled=True)]
    dynamic_update_slice x48 -> x0, other arithmetic: 71.4 us -> none  [accumulate(): lax.dynamic_update_slice(accumulator, updated, (row_start, col_start))]
    dot_general x26 -> x0, matrix products: 50.4 us -> none  [the longest x12 18.8 us: schur_rows(): jnp.dot(coupled[item_index], full_panel, precision=HIGHEST_PRECISION, pre...]
    another operation x1 -> x0, loops' own time: 39.1 us -> none  [on_device(): accumulator = lax.fori_loop(0, item_count, accumulate, accumulator)]
    psum x1 -> x0, waiting for transfers between devices: 32.4 us -> none  [on_device(): coupled = lax.psum(coupled_local, 'camera')]
    all_gather x1 -> x0, waiting for transfers between devices: 30.6 us -> none  [on_device(): full_jac = lax.all_gather(masked, 'camera', axis=2, tiled=True)]
    ppermute x3 -> x0, waiting for transfers between devices: 27.1 us -> none  [passed_along(): return lax.ppermute(block, axis, route)]
  transfers between devices with their start and end apart: 6 -> 0, of which waited for: 4 -> 0; matrix products, arithmetic and copies ran while one was open for 9% -> 0% of each run, Pallas kernels for 0% -> 0%
where the time goes in v1:
time: 113 us
  Pallas kernels  104 us (92%)
  local copies, waits for them, and re-layouts  9.4 us (8%)
    pallas_call x1, Pallas kernels, reduce(): pl.pallas_call(functools.partial(reduce_kernel, bits, parts, group_tiles)...  51.7 us
    pallas_call x1, Pallas kernels, exchange(): pl.pallas_call(exchange_kernel, name='camera_exchange', out_shape=(jax.Sh...  41.8 us
    pallas_call x1, Pallas kernels, schur(): pl.pallas_call(functools.partial(schur_kernel, group_tiles), name='schur_...  10.2 us
    unnamed x8, local copies, waits for them, and re-layouts  8.71 us

profile of v1, /device:TPU:0, one launch (start us, length us, event | category | flops | bytes accessed | tf_op | source)
XLA Modules:
  0.0 113.2 jit_solution(5910683474479939846)
XLA Ops:
  0.0 0.0 copy-start
  0.0 6.0 %copy.9.points = f32[16,128,3,128]{3,2,1,0:T(4,128)} copy(f32[16,128,3,128]{3,1,2,0:T(8,128)} %param.8) | data formatting | bytes 6291456 | tf_op args[3]
  6.0 0.0 copy-done
  6.0 0.0 copy-start.1
  6.0 0.7 copy.10.inv
  6.7 41.8 %camera_exchange.1 = (f32[3,16,128,128]{3,2,1,0:T(8,128)}, f32[16,128,128]{2,1,0:T(8,128)}) custom-call(f32[16,128,128]{2,1,0:T(8,128)} %jac.3, f32[16,128,3,128]{3,2,1,0:T(4,128)} %copy.9.points, f32[16,3,3,128]{3,2,1,0:T(4,128)} %copy.10.inv), custom_call_target="tpu_custom_call" | custom-call | tf_op jit(solution)/shard_map/camera_exchange/pallas_call | solution.py:120
  48.6 0.0 copy-done.1
  48.6 0.1 copy.8
  48.7 0.7 reshape.6.tiles
  49.4 10.2 %schur_sum.1 = f32[512,1664]{1,0:T(8,128)} custom-call(s32[8]{0:T(128)} %counts.1, s32[512]{0:T(512)} %reshape.6.tiles, f32[16,128,128]{2,1,0:T(8,128)} %jac.3, f32[3,16,128,128]{3,2,1,0:T(8,128)} %get-tuple-element.7.others, f32[16,128,128]{2,1,0:T(8,128)} %get-tuple-element.8.coupled), custom_call_target="tpu_custom_call" | custom-call | tf_op jit(solution)/shard_map/schur_sum/pallas_call | solution.py:178
  59.5 51.7 %cluster_reduce.1 = f32[64,2048]{1,0:T(8,128)} custom-call(f32[2,2,2,64,1664]{4,3,2,1,0:T(8,128)} %bitcast.2), custom_call_target="tpu_custom_call" | custom-call | tf_op jit(solution)/shard_map/cluster_reduce/pallas_call | solution.py:276
  111.3 1.9 %copy.12 = f32[1,64,2048]{2,1,0:T(8,128)} copy(f32[1,64,2048]{2,1,0:T(8,128)} %bitcast.3) | data formatting | bytes 1048576
Async XLA Ops:
  0.0 6.0 %copy-start = (f32[16,3,3,128]{3,0,2,1:T(8,128)S(1)}, f32[16,3,3,128]{3,0,2,1:T(8,128)}, u32[]{:S(2)}) copy-start(f32[16,3,3,128]{3,0,2,1:T(8,128)} %param.9) | copy-start | bytes 221188
  6.0 42.5 %copy-start.1 = (s32[128,4]{0,1:T(4,128)S(1)}, s32[128,4]{0,1:T(4,128)}, u32[]{:S(2)}) copy-start(s32[128,4]{0,1:T(4,128)} %param.6) | copy-start | bytes 6148

commit v2 on v1

v2 whole, which is shorter than its diff:
```python
import functools
import itertools

import jax
import jax.numpy as jnp
from jax import lax
from jax.experimental import pallas as pl
from jax.experimental.pallas import tpu as pltpu
from jax.sharding import PartitionSpec as P

MESH = pl.DeviceIdType.MESH
ANY = pl.BlockSpec(memory_space=pl.ANY)
VMEM = pl.BlockSpec(memory_space=pltpu.VMEM)
SMEM = pl.BlockSpec(memory_space=pltpu.SMEM)
LANES = 128
GROUP_TILES = 4
VMEM_LIMIT = 56 * 1024 * 1024


def halves(x):
    high = x.astype(jnp.bfloat16)
    low = (x - high.astype(jnp.float32)).astype(jnp.bfloat16)
    return high, low


def dot3(left, right, dims):
    lh, ll = halves(left)
    rh, rl = halves(right)
    (ld,), (rd,) = dims
    return lax.dot_general(
        jnp.concatenate([lh, lh, ll], axis=ld),
        jnp.concatenate([rh, rl, rh], axis=rd),
        (dims, ((), ())),
        preferred_element_type=jnp.float32,
    )


def greet(peers):
    barrier = pltpu.get_barrier_semaphore()
    for peer in peers:
        pl.semaphore_signal(barrier, inc=1, device_id=peer, device_id_type=MESH)
    pl.semaphore_wait(barrier, len(peers))


def send(src, dst, send_sem, recv_sem, peer):
    return pltpu.make_async_remote_copy(
        src_ref=src, dst_ref=dst, send_sem=send_sem, recv_sem=recv_sem,
        device_id=peer, device_id_type=MESH,
    )


def exchange_kernel(
    jac, points, inv, near, far, coupled,
    points_here, outgoing, arrived, mine, across_in,
    send_sem, recv_sem, local_sem,
):
    camera = lax.axis_index("camera")
    core = lax.rem(camera, 2)
    sibling = {"camera": camera + 1 - 2 * core}
    across = {"camera": lax.rem(camera + 2, 4)}
    half = coupled.shape[0] // 2
    own, theirs = core * half, (1 - core) * half

    loads = [
        pltpu.make_async_copy(
            points.at[pl.ds(start, half)], points_here.at[which], local_sem.at[which]
        )
        for which, start in enumerate((theirs, own))
    ]
    for load in loads:
        load.start()
    greet([sibling, across])
    early = jac.at[pl.ds(0, far.shape[1])]
    to_across = send(early, far.at[0], send_sem.at[0], recv_sem.at[0], across)
    to_across.start()
    to_sibling = send(jac, near, send_sem.at[1], recv_sem.at[1], sibling)
    to_sibling.start()

    def couple(which, start, target):
        def body(i, carry):
            p = [points_here[which, i, j] for j in range(3)]
            w = [
                sum(p[j] * inv[j, k, pl.ds(start + i, 1), :] for j in range(3))
                for k in range(3)
            ]
            target[i] = dot3(
                jnp.concatenate(w, axis=1), jnp.concatenate(p, axis=1), (((1,), (1,)))
            )
            return carry

        loads[which].wait()
        lax.fori_loop(0, half, body, 0)

    couple(0, theirs, outgoing)
    part = send(outgoing, arrived, send_sem.at[2], recv_sem.at[2], sibling)
    part.start()
    couple(1, own, mine)
    part.wait_recv()
    mine[...] += arrived[...]
    cross = send(mine, across_in, send_sem.at[3], recv_sem.at[3], across)
    cross.start()
    to_across.wait_recv()
    forward = send(far.at[0], far.at[1], send_sem.at[4], recv_sem.at[4], sibling)
    forward.start()
    cross.wait_recv()
    block = coupled.at[pl.ds(own, half)]
    block[...] = mine[...] + across_in[...]
    back = send(block, block, send_sem.at[5], recv_sem.at[5], sibling)
    back.start()
    for copy in (to_across, to_sibling, part, cross):
        copy.wait_send()
    to_sibling.wait_recv()
    forward.wait()
    back.wait()


def exchange(jac, points, inv):
    slots, rows, width = jac.shape
    half = slots // 2
    block = pltpu.VMEM((half, rows, rows), jnp.float32)
    return pl.pallas_call(
        exchange_kernel,
        name="camera_exchange",
        out_shape=(
            jax.ShapeDtypeStruct((slots, rows, width), jnp.float32),
            jax.ShapeDtypeStruct((2, half, rows, width), jnp.float32),
            jax.ShapeDtypeStruct((slots, rows, rows), jnp.float32),
        ),
        in_specs=[ANY, ANY, VMEM],
        out_specs=(ANY, ANY, VMEM),
        scratch_shapes=[
            pltpu.VMEM((2, half) + points.shape[1:], jnp.float32),
            block, block, block, block,
            pltpu.SemaphoreType.DMA((6,)),
            pltpu.SemaphoreType.DMA((6,)),
            pltpu.SemaphoreType.DMA((2,)),
        ],
        compiler_params=pltpu.CompilerParams(
            collective_id=0, has_side_effects=True, vmem_limit_bytes=VMEM_LIMIT
        ),
    )(jac, points, inv)


def add_pair(tiles, acc, slot, camera, r, first, width, block):
    other = jnp.bitwise_xor(camera, r)
    row_tile, col_tile = tiles[camera, slot], tiles[other, slot]
    upper = (camera > other).astype(jnp.int32)

    @pl.when(lax.rem(row_tile + col_tile + upper, 2) == 0)
    def _():
        row = pl.ds(pl.multiple_of(row_tile * width, width), width)
        col = pl.multiple_of(first + (col_tile // 2) * width, width)
        acc[row, pl.ds(col, width)] += block


def near_kernel(counts, tiles, jac, near, coupled, acc, left):
    camera = lax.axis_index("camera")
    device = lax.axis_index("cluster")
    slots, _, width = jac.shape
    live = counts[device]
    acc[...] = jnp.zeros_like(acc)

    def one(c):
        panel = jac[c]
        schur = panel - dot3(coupled[c], panel, (((1,), (0,))))
        schur = schur * jnp.where(c < live, 1.0, 0.0)
        left[c] = schur
        return dot3(schur, jnp.concatenate([panel, near[c]], axis=1), (((0,), (0,))))

    def add(c, block):
        slot = device * slots + c
        row = pl.ds(pl.multiple_of(tiles[camera, slot] * width, width), width)
        acc[row, :width] += block[:, :width]
        add_pair(tiles, acc, slot, camera, 1, width, width, block[:, width:])

    def body(step, carry):
        blocks = [one(2 * step), one(2 * step + 1)]
        add(2 * step, blocks[0])
        add(2 * step + 1, blocks[1])
        return carry

    lax.fori_loop(0, (live + 1) // 2, body, 0)


def near_sum(counts, tiles, jac, near, coupled):
    slots, rows, width = jac.shape
    return pl.pallas_call(
        near_kernel,
        name="near_sum",
        out_shape=(
            jax.ShapeDtypeStruct(
                (GROUP_TILES * width, (1 + GROUP_TILES // 2) * width), jnp.float32
            ),
            jax.ShapeDtypeStruct((slots, rows, width), jnp.float32),
        ),
        in_specs=[SMEM, SMEM, VMEM, VMEM, VMEM],
        out_specs=(VMEM, VMEM),
        compiler_params=pltpu.CompilerParams(vmem_limit_bytes=VMEM_LIMIT),
    )(counts, tiles, jac, near, coupled)


def far_kernel(counts, tiles, left, early, late, acc):
    camera = lax.axis_index("camera")
    device = lax.axis_index("cluster")
    slots, _, width = left.shape
    half = early.shape[1]
    live = counts[device]
    acc[...] = jnp.zeros_like(acc)

    def part(far, base, steps):
        def one(i):
            right = jnp.concatenate([far[0, i], far[1, i]], axis=1)
            return dot3(left[base + i], right, (((0,), (0,))))

        def add(i, block):
            slot = device * slots + base + i
            for r in (2, 3):
                cut = block[:, (r - 2) * width:(r - 1) * width]
                first = (r - 2) * (GROUP_TILES // 2) * width
                add_pair(tiles, acc, slot, camera, r, first, width, cut)

        def body(step, carry):
            blocks = [one(2 * step), one(2 * step + 1)]
            add(2 * step, blocks[0])
            add(2 * step + 1, blocks[1])
            return carry

        lax.fori_loop(0, steps, body, 0)

    steps = (live + 1) // 2
    part(early, 0, jnp.minimum(steps, half // 2))
    part(late, half, jnp.maximum(steps - half // 2, 0))


def far_sum(counts, tiles, left, early, late):
    width = left.shape[2]
    return pl.pallas_call(
        far_kernel,
        name="far_sum",
        out_shape=jax.ShapeDtypeStruct(
            (GROUP_TILES * width, GROUP_TILES * width), jnp.float32
        ),
        in_specs=[SMEM, SMEM, VMEM, VMEM, VMEM],
        out_specs=VMEM,
        compiler_params=pltpu.CompilerParams(vmem_limit_bytes=VMEM_LIMIT),
    )(counts, tiles, left, early, late)


class Reduction:
    def __init__(self, bits, width, orders, given, acc, buffers, sems):
        self.bits, self.width, self.orders = bits, width, orders
        self.given, self.acc, self.buffers = given, acc, buffers
        self.send_sem, self.recv_sem, self.local_sem = sems
        device = lax.axis_index("cluster")
        self.bit = [lax.rem(device // (1 << b), 2) for b in range(bits)]
        self.peers = [
            {"cluster": device + (1 - 2 * self.bit[b]) * (1 << b)} for b in range(bits)
        ]
        self.copies = {}

    def load(self):
        self.loads = []
        for part in range(len(self.orders)):
            at = (slice(None),) * (self.bits + 1) + (self.columns(part),)
            copy = pltpu.make_async_copy(
                self.given.at[at], self.acc.at[at], self.local_sem.at[part]
            )
            copy.start()
            self.loads.append(copy)

    def columns(self, part):
        return pl.ds(part * self.width, self.width)

    def region(self, part, step, flip):
        index = [slice(None)] * self.bits
        order = self.orders[part]
        for b in order[:step]:
            index[self.bits - 1 - b] = self.bit[b]
        b = order[step]
        index[self.bits - 1 - b] = 1 - self.bit[b] if flip else self.bit[b]
        return index

    def start(self, part, step):
        which = part * self.bits + step
        source = self.acc if step else self.given
        index = tuple(self.region(part, step, True))
        copy = send(
            source.at[index + (slice(None), self.columns(part))], self.buffers[which],
            self.send_sem.at[which], self.recv_sem.at[which],
            self.peers[self.orders[part][step]],
        )
        copy.start()
        self.copies[part, step] = copy

    def begin(self):
        for part in range(len(self.orders)):
            self.start(part, 0)

    def run(self, finished):
        for step in range(self.bits):
            for part in range(len(self.orders)):
                if step == 0:
                    self.loads[part].wait()
                self.copies[part, step].wait_recv()
                index = self.region(part, step, False)
                free = [i for i in range(self.bits) if isinstance(index[i], slice)]
                for place in itertools.product(range(2), repeat=len(free)):
                    full = list(index)
                    for i, value in zip(free, place):
                        full[i] = value
                    at = tuple(full) + (slice(None), self.columns(part))
                    self.acc[at] += self.buffers[part * self.bits + step][place]
                if step + 1 < self.bits:
                    self.start(part, step + 1)
                else:
                    finished(part, tuple(reversed(self.bit)) + (slice(None), self.columns(part)))

    def end(self):
        for copy in self.copies.values():
            copy.wait_send()


def reduction_scratch(bits, rows, width, parts):
    count = parts * bits
    return (
        [pltpu.VMEM((2,) * bits + (rows, parts * width), jnp.float32)]
        + [
            pltpu.VMEM((2,) * (bits - 1 - step) + (rows, width), jnp.float32)
            for _ in range(parts)
            for step in range(bits)
        ]
        + [pltpu.SemaphoreType.DMA((n,)) for n in (count, count, parts)]
    )


def orders_of(bits, parts):
    straight = tuple(range(bits))
    swapped = (1, 0) + straight[2:]
    return [swapped if part == 1 else straight for part in range(parts)]


def near_reduce_kernel(bits, width, given, jac, out, far, acc, *scratch):
    parts = out.shape[1] // width
    buffers, sems = scratch[:parts * bits], scratch[parts * bits:-2]
    send_sem, recv_sem = scratch[-2:]
    camera = lax.axis_index("camera")
    sibling = {"camera": camera + 1 - 2 * lax.rem(camera, 2)}
    across = {"camera": lax.rem(camera + 2, 4)}
    work = Reduction(bits, width, orders_of(bits, parts), given, acc, buffers, sems)
    work.load()
    greet(work.peers + [sibling, across])
    work.begin()
    late = far.shape[1]
    to_across = send(
        jac.at[pl.ds(jac.shape[0] - late, late)], far.at[0],
        send_sem.at[0], recv_sem.at[0], across,
    )
    to_across.start()

    def finished(part, at):
        out[:, part * width:(part + 1) * width] = acc[at]

    work.run(finished)
    to_across.wait_recv()
    forward = send(far.at[0], far.at[1], send_sem.at[1], recv_sem.at[1], sibling)
    forward.start()
    work.end()
    to_across.wait_send()
    forward.wait()


def near_reduce(acc, jac, devices):
    wide, columns = acc.shape
    slots, depth, width = jac.shape
    bits = devices.bit_length() - 1
    rows = wide // devices
    return pl.pallas_call(
        functools.partial(near_reduce_kernel, bits, width),
        name="near_reduce",
        out_shape=(
            jax.ShapeDtypeStruct((rows, columns), jnp.float32),
            jax.ShapeDtypeStruct((2, slots - slots // 2, depth, width), jnp.float32),
        ),
        in_specs=[ANY, ANY],
        out_specs=(VMEM, ANY),
        scratch_shapes=reduction_scratch(bits, rows, width, columns // width)
        + [pltpu.SemaphoreType.DMA((2,)), pltpu.SemaphoreType.DMA((2,))],
        compiler_params=pltpu.CompilerParams(
            collective_id=1, has_side_effects=True, vmem_limit_bytes=VMEM_LIMIT
        ),
    )(acc.reshape((2,) * bits + (rows, columns)), jac)


def far_reduce_kernel(bits, width, given, near, out, acc, *scratch):
    parts = GROUP_TILES
    pairs = GROUP_TILES // 2
    buffers, sems = scratch[:parts * bits], scratch[parts * bits:-4]
    strips, traded, send_sem, recv_sem = scratch[-4:]
    camera = lax.axis_index("camera")
    device = lax.axis_index("cluster")
    rows = out.shape[0]
    shares = width // rows
    tile, place = device // shares, lax.rem(device, shares)
    work = Reduction(bits, width, orders_of(bits, parts), given, acc, buffers, sems)
    work.load()

    other = [jnp.bitwise_xor(camera, r) for r in range(4)]
    parity = [lax.rem(tile + (camera > other[r]).astype(jnp.int32), 2) for r in range(4)]
    barrier = pltpu.get_barrier_semaphore()
    for peer in work.peers:
        pl.semaphore_signal(barrier, inc=1, device_id=peer, device_id_type=MESH)
    for r in range(1, 4):
        for k in range(pairs):
            for d in range(shares):
                peer = {
                    "camera": other[r], "cluster": (2 * k + 1 - parity[r]) * shares + d
                }
                pl.semaphore_signal(barrier, inc=1, device_id=peer, device_id_type=MESH)
    pl.semaphore_wait(barrier, bits + 3 * pairs * shares)

    trades = []

    def trade(r, k):
        for d in range(shares):
            copy = send(
                strips.at[r - 1, k],
                traded.at[r - 1, tile // 2, pl.ds(place * rows, rows)],
                send_sem.at[((r - 1) * pairs + k) * shares + d], recv_sem.at[r - 1],
                {"camera": other[r], "cluster": (2 * k + parity[r]) * shares + d},
            )
            copy.start()
            trades.append(copy)

    def column(r, t):
        return pl.ds(pl.multiple_of((other[r] * GROUP_TILES + t) * width, width), width)

    work.begin()
    for k in range(pairs):
        strips[0, k] = near[:, (1 + k) * width:(2 + k) * width]
        trade(1, k)
    for t in range(GROUP_TILES):
        out[:, column(0, t)] = jnp.where(t == tile, near[:, :width], 0.0)

    def finished(part, at):
        r, k = 2 + part // pairs, part % pairs
        strips[r - 1, k] = acc[at]
        trade(r, k)

    work.run(finished)
    for r in range(1, 4):
        pltpu.make_async_copy(traded.at[r - 1], traded.at[r - 1], recv_sem.at[r - 1]).wait()
        for k in range(pairs):
            out[:, column(r, 2 * k + parity[r])] = strips[r - 1, k]
            turned = traded[r - 1, k].T
            kept = turned[:rows]
            for d in range(1, shares):
                kept = jnp.where(place == d, turned[d * rows:(d + 1) * rows], kept)
            out[:, column(r, 2 * k + 1 - parity[r])] = kept
    work.end()
    for copy in trades:
        copy.wait_send()


def far_reduce(acc, near, devices, cameras, width):
    wide, columns = acc.shape
    bits = devices.bit_length() - 1
    rows = wide // devices
    pairs = GROUP_TILES // 2
    return pl.pallas_call(
        functools.partial(far_reduce_kernel, bits, width),
        name="far_reduce",
        out_shape=jax.ShapeDtypeStruct((rows, cameras * wide), jnp.float32),
        in_specs=[ANY, VMEM],
        out_specs=VMEM,
        scratch_shapes=reduction_scratch(bits, rows, width, columns // width)
        + [
            pltpu.VMEM((3, pairs, rows, width), jnp.float32),
            pltpu.VMEM((3, pairs, width, width), jnp.float32),
            pltpu.SemaphoreType.DMA((3 * pairs * width // rows,)),
            pltpu.SemaphoreType.DMA((3,)),
        ],
        compiler_params=pltpu.CompilerParams(
            collective_id=2, has_side_effects=True, vmem_limit_bytes=VMEM_LIMIT
        ),
    )(acc.reshape((2,) * bits + (rows, columns)), near)


def on_device(counts, tiles, cam_jac, point_jac, point_inv):
    devices = lax.axis_size("cluster")
    cameras = lax.axis_size("camera")
    width = cam_jac.shape[2]
    tiles = tiles.T
    near, early, coupled = exchange(
        cam_jac, point_jac.transpose(0, 2, 1, 3), point_inv.transpose(1, 2, 0, 3)
    )
    near_acc, left = near_sum(counts, tiles, cam_jac, near, coupled)
    near_strip, late = near_reduce(near_acc, cam_jac, devices)
    far_acc = far_sum(counts, tiles, left, early, late)
    return far_reduce(far_acc, near_strip, devices, cameras, width)[None]


def solution(mesh):
    in_specs = (
        P(),
        P(),
        P("cluster", None, "camera"),
        P("cluster", None, None, "camera"),
        P("cluster", None, None, "camera"),
    )
    out_specs = P("camera", "cluster", None)
    return jax.shard_map(
        on_device,
        mesh=mesh, in_specs=in_specs, out_specs=out_specs, check_vma=False,
    )
```

time: 113 us -> 97.4 us (0.86)
  Pallas kernels: 104 us -> 94.7 us
  local copies, waits for them, and re-layouts: 9.4 us -> 1.87 us
    pallas_call x1, Pallas kernels: 41.8 us -> 30.6 us  [exchange(): pl.pallas_call(exchange_kernel, name='camera_exchange', out_shape=(jax.Sh...]
    unnamed x8 -> x1, local copies, waits for them, and re-layouts: 8.71 us -> 1.87 us
    pallas_call x2 -> x4, Pallas kernels: 61.9 us -> 64.1 us  [the longest x1 30.7 us: far_reduce(): pl.pallas_call(functools.partial(far_reduce_kernel, bits, width), name='f...]
where the time goes in v2:
time: 97.4 us; the launch traced here: 96.6 us
  Pallas kernels  94.7 us (97%)
  local copies, waits for them, and re-layouts  1.87 us (2%)
    pallas_call x1, Pallas kernels, far_reduce(): pl.pallas_call(functools.partial(far_reduce_kernel, bits, width), name='f...  30.7 us
    pallas_call x1, Pallas kernels, exchange(): pl.pallas_call(exchange_kernel, name='camera_exchange', out_shape=(jax.Sh...  30.6 us
    pallas_call x1, Pallas kernels, near_reduce(): pl.pallas_call(functools.partial(near_reduce_kernel, bits, width), name='...  26.3 us
    pallas_call x1, Pallas kernels, near_sum(): pl.pallas_call(near_kernel, name='near_sum', out_shape=(jax.ShapeDtypeStr...  3.9 us
    pallas_call x1, Pallas kernels, far_sum(): pl.pallas_call(far_kernel, name='far_sum', out_shape=jax.ShapeDtypeStruct...  3.25 us

profile of v2, /device:TPU:0, one launch (start us, length us, event | category | flops | bytes accessed | tf_op | source)
XLA Modules:
  0.0 96.6 jit_solution(7215284952542998848)
XLA Ops:
  0.0 30.6 %camera_exchange.1 = (f32[16,128,128]{2,1,0:T(8,128)}, f32[2,8,128,128]{3,2,1,0:T(8,128)}, f32[16,128,128]{2,1,0:T(8,128)}) custom-call(f32[16,128,128]{2,1,0:T(8,128)} %jac.5, f32[16,3,128,128]{3,2,1,0:T(8,128)} %bitcast.7, f32[3,3,16,128]{3,2,1,0:T(8,128)} %bitcast.10), custom_call_target="tpu_custom_call" | custom-call | tf_op jit(solution)/shard_map/camera_exchange/pallas_call | solution.py:121
  30.6 3.9 %near_sum.1 = (f32[512,384]{1,0:T(8,128)}, f32[16,128,128]{2,1,0:T(8,128)}) custom-call(s32[8]{0:T(128)} %counts.3, s32[4,128]{1,0:T(4,128)} %bitcast.11, f32[16,128,128]{2,1,0:T(8,128)} %jac.5, f32[16,128,128]{2,1,0:T(8,128)} %get-tuple-element.12.near, f32[16,128,128]{2,1,0:T(8,128)} %get-tuple-element.13.coupled), custom_call_target="tpu_custom_call" | custom-call | tf_op jit(solution)/shard_map/near_sum/pallas_call | solution.py:187
  34.5 26.3 %near_reduce.1 = (f32[64,384]{1,0:T(8,128)}, f32[2,8,128,128]{3,2,1,0:T(8,128)}) custom-call(f32[2,2,2,64,384]{4,3,2,1,0:T(8,128)} %bitcast.9, f32[16,128,128]{2,1,0:T(8,128)} %jac.5), custom_call_target="tpu_custom_call" | custom-call | tf_op jit(solution)/shard_map/near_reduce/pallas_call | solution.py:377
  60.8 3.2 %far_sum.1 = f32[512,512]{1,0:T(8,128)} custom-call(s32[8]{0:T(128)} %counts.3, s32[4,128]{1,0:T(4,128)} %bitcast.12, f32[16,128,128]{2,1,0:T(8,128)} %get-tuple-element.14.left, f32[2,8,128,128]{3,2,1,0:T(8,128)} %get-tuple-element.15.early, f32[2,8,128,128]{3,2,1,0:T(8,128)} %get-tuple-element.17.late), custom_call_target="tpu_custom_call" | custom-call | tf_op jit(solution)/shard_map/far_sum/pallas_call | solution.py:237
  64.0 30.7 %far_reduce.1 = f32[64,2048]{1,0:T(8,128)} custom-call(f32[2,2,2,64,512]{4,3,2,1,0:T(8,128)} %bitcast.6, f32[64,384]{1,0:T(8,128)} %get-tuple-element.18.near), custom_call_target="tpu_custom_call" | custom-call | tf_op jit(solution)/shard_map/far_reduce/pallas_call | solution.py:469
  94.7 1.9 %copy.7 = f32[1,64,2048]{2,1,0:T(8,128)} copy(f32[1,64,2048]{2,1,0:T(8,128)} %bitcast.8) | data formatting | bytes 1048576

commit v3 on v2

--- a/solution.py
+++ b/solution.py
@@ -14,6 +14,8 @@
 SMEM = pl.BlockSpec(memory_space=pltpu.SMEM)
 LANES = 128
 GROUP_TILES = 4
+STRIDE = 4
+CHUNKS = 3
 VMEM_LIMIT = 56 * 1024 * 1024
 
 
@@ -59,81 +61,86 @@
     sibling = {"camera": camera + 1 - 2 * core}
     across = {"camera": lax.rem(camera + 2, 4)}
     half = coupled.shape[0] // 2
+    quarter = half // 2
     own, theirs = core * half, (1 - core) * half
+    starts = [theirs, own, theirs + quarter, own + quarter]
 
     loads = [
         pltpu.make_async_copy(
-            points.at[pl.ds(start, half)], points_here.at[which], local_sem.at[which]
+            points.at[pl.ds(start, quarter)], points_here.at[which], local_sem.at[which]
         )
-        for which, start in enumerate((theirs, own))
+        for which, start in enumerate(starts)
     ]
     for load in loads:
         load.start()
     greet([sibling, across])
-    early = jac.at[pl.ds(0, far.shape[1])]
-    to_across = send(early, far.at[0], send_sem.at[0], recv_sem.at[0], across)
-    to_across.start()
-    to_sibling = send(jac, near, send_sem.at[1], recv_sem.at[1], sibling)
-    to_sibling.start()
-
-    def couple(which, start, target):
+
+    def copy_to(which, src, dst, peer):
+        copy = send(src, dst, send_sem.at[which], recv_sem.at[which], peer)
+        copy.start()
+        return copy
+
+    to_across = copy_to(0, jac.at[pl.ds(0, far.shape[1])], far.at[0], across)
+    to_sibling = copy_to(1, jac, near, sibling)
+
+    def couple(which, target):
         def body(i, carry):
             p = [points_here[which, i, j] for j in range(3)]
             w = [
-                sum(p[j] * inv[j, k, pl.ds(start + i, 1), :] for j in range(3))
+                sum(p[j] * inv[j, k, pl.ds(starts[which] + i, 1), :] for j in range(3))
                 for k in range(3)
             ]
-            target[i] = dot3(
+            target[which // 2, i] = dot3(
                 jnp.concatenate(w, axis=1), jnp.concatenate(p, axis=1), (((1,), (1,)))
             )
             return carry
 
         loads[which].wait()
-        lax.fori_loop(0, half, body, 0)
-
-    couple(0, theirs, outgoing)
-    part = send(outgoing, arrived, send_sem.at[2], recv_sem.at[2], sibling)
-    part.start()
-    couple(1, own, mine)
-    part.wait_recv()
-    mine[...] += arrived[...]
-    cross = send(mine, across_in, send_sem.at[3], recv_sem.at[3], across)
-    cross.start()
+        lax.fori_loop(0, quarter, body, 0, unroll=2)
+
+    sent, crossed, returned = [], [], []
+    for q in range(2):
+        couple(2 * q, outgoing)
+        sent.append(copy_to(2 + q, outgoing.at[q], arrived.at[q], sibling))
+        couple(2 * q + 1, mine)
+        sent[q].wait_recv()
+        mine[q] += arrived[q]
+        crossed.append(copy_to(4 + q, mine.at[q], across_in.at[q], across))
     to_across.wait_recv()
-    forward = send(far.at[0], far.at[1], send_sem.at[4], recv_sem.at[4], sibling)
-    forward.start()
-    cross.wait_recv()
-    block = coupled.at[pl.ds(own, half)]
-    block[...] = mine[...] + across_in[...]
-    back = send(block, block, send_sem.at[5], recv_sem.at[5], sibling)
-    back.start()
-    for copy in (to_across, to_sibling, part, cross):
+    forward = copy_to(6, far.at[0], far.at[1], sibling)
+    for q in range(2):
+        crossed[q].wait_recv()
+        block = coupled.at[pl.ds(own + q * quarter, quarter)]
+        block[...] = mine[q] + across_in[q]
+        returned.append(copy_to(7 + q, block, block, sibling))
+    for copy in [to_across, to_sibling] + sent + crossed:
         copy.wait_send()
     to_sibling.wait_recv()
     forward.wait()
-    back.wait()
+    for copy in returned:
+        copy.wait()
 
 
 def exchange(jac, points, inv):
     slots, rows, width = jac.shape
-    half = slots // 2
-    block = pltpu.VMEM((half, rows, rows), jnp.float32)
+    quarter = slots // 4
+    block = pltpu.VMEM((2, quarter, rows, rows), jnp.float32)
     return pl.pallas_call(
         exchange_kernel,
         name="camera_exchange",
         out_shape=(
             jax.ShapeDtypeStruct((slots, rows, width), jnp.float32),
-            jax.ShapeDtypeStruct((2, half, rows, width), jnp.float32),
+            jax.ShapeDtypeStruct((2, quarter, rows, width), jnp.float32),
             jax.ShapeDtypeStruct((slots, rows, rows), jnp.float32),
         ),
         in_specs=[ANY, ANY, VMEM],
         out_specs=(ANY, ANY, VMEM),
         scratch_shapes=[
-            pltpu.VMEM((2, half) + points.shape[1:], jnp.float32),
+            pltpu.VMEM((4, quarter) + points.shape[1:], jnp.float32),
             block, block, block, block,
-            pltpu.SemaphoreType.DMA((6,)),
-            pltpu.SemaphoreType.DMA((6,)),
-            pltpu.SemaphoreType.DMA((2,)),
+            pltpu.SemaphoreType.DMA((9,)),
+            pltpu.SemaphoreType.DMA((9,)),
+            pltpu.SemaphoreType.DMA((4,)),
         ],
         compiler_params=pltpu.CompilerParams(
             collective_id=0, has_side_effects=True, vmem_limit_bytes=VMEM_LIMIT
@@ -174,12 +181,12 @@
         add_pair(tiles, acc, slot, camera, 1, width, width, block[:, width:])
 
     def body(step, carry):
-        blocks = [one(2 * step), one(2 * step + 1)]
-        add(2 * step, blocks[0])
-        add(2 * step + 1, blocks[1])
+        blocks = [one(STRIDE * step + i) for i in range(STRIDE)]
+        for i in range(STRIDE):
+            add(STRIDE * step + i, blocks[i])
         return carry
 
-    lax.fori_loop(0, (live + 1) // 2, body, 0)
+    lax.fori_loop(0, (live + STRIDE - 1) // STRIDE, body, 0)
 
 
 def near_sum(counts, tiles, jac, near, coupled):
@@ -203,7 +210,7 @@
     camera = lax.axis_index("camera")
     device = lax.axis_index("cluster")
     slots, _, width = left.shape
-    half = early.shape[1]
+    first = early.shape[1]
     live = counts[device]
     acc[...] = jnp.zeros_like(acc)
 
@@ -216,20 +223,20 @@
             slot = device * slots + base + i
             for r in (2, 3):
                 cut = block[:, (r - 2) * width:(r - 1) * width]
-                first = (r - 2) * (GROUP_TILES // 2) * width
-                add_pair(tiles, acc, slot, camera, r, first, width, cut)
+                column = (r - 2) * (GROUP_TILES // 2) * width
+                add_pair(tiles, acc, slot, camera, r, column, width, cut)
 
         def body(step, carry):
-            blocks = [one(2 * step), one(2 * step + 1)]
-            add(2 * step, blocks[0])
-            add(2 * step + 1, blocks[1])
+            blocks = [one(STRIDE * step + i) for i in range(STRIDE)]
+            for i in range(STRIDE):
+                add(STRIDE * step + i, blocks[i])
             return carry
 
         lax.fori_loop(0, steps, body, 0)
 
-    steps = (live + 1) // 2
-    part(early, 0, jnp.minimum(steps, half // 2))
-    part(late, half, jnp.maximum(steps - half // 2, 0))
+    steps = (live + STRIDE - 1) // STRIDE
+    part(early, 0, jnp.minimum(steps, first // STRIDE))
+    part(late, first, jnp.maximum(steps - first // STRIDE, 0))
 
 
 def far_sum(counts, tiles, left, early, late):
@@ -296,7 +303,7 @@
         for part in range(len(self.orders)):
             self.start(part, 0)
 
-    def run(self, finished):
+    def run(self, finished, between=lambda step: None):
         for step in range(self.bits):
             for part in range(len(self.orders)):
                 if step == 0:
@@ -314,6 +321,7 @@
                     self.start(part, step + 1)
                 else:
                     finished(part, tuple(reversed(self.bit)) + (slice(None), self.columns(part)))
+            between(step)
 
     def end(self):
         for copy in self.copies.values():
@@ -336,7 +344,10 @@
 def orders_of(bits, parts):
     straight = tuple(range(bits))
     swapped = (1, 0) + straight[2:]
-    return [swapped if part == 1 else straight for part in range(parts)]
+    far_first = (bits - 1,) + straight[:-1]
+    if parts % 2:
+        return [(straight, swapped, far_first)[part % 3] for part in range(parts)]
+    return [(straight, swapped)[part % 2] for part in range(parts)]
 
 
 def near_reduce_kernel(bits, width, given, jac, out, far, acc, *scratch):
@@ -351,22 +362,40 @@
     greet(work.peers + [sibling, across])
     work.begin()
     late = far.shape[1]
-    to_across = send(
-        jac.at[pl.ds(jac.shape[0] - late, late)], far.at[0],
-        send_sem.at[0], recv_sem.at[0], across,
-    )
-    to_across.start()
+    chunk = late // CHUNKS
+    to_across, forwards = [], []
+    for i in range(CHUNKS):
+        to_across.append(send(
+            jac.at[pl.ds(jac.shape[0] - late + i * chunk, chunk)],
+            far.at[0, pl.ds(i * chunk, chunk)],
+            send_sem.at[i], recv_sem.at[i], across,
+        ))
+        to_across[i].start()
+
+    def forward(i):
+        to_across[i].wait_recv()
+        part = pl.ds(i * chunk, chunk)
+        forwards.append(send(
+            far.at[0, part], far.at[1, part],
+            send_sem.at[CHUNKS + i], recv_sem.at[CHUNKS + i], sibling,
+        ))
+        forwards[i].start()
 
     def finished(part, at):
         out[:, part * width:(part + 1) * width] = acc[at]
 
-    work.run(finished)
-    to_across.wait_recv()
-    forward = send(far.at[0], far.at[1], send_sem.at[1], recv_sem.at[1], sibling)
-    forward.start()
+    def between(step):
+        if 1 <= step <= CHUNKS:
+            forward(step - 1)
+
+    work.run(finished, between)
+    for i in range(len(forwards), CHUNKS):
+        forward(i)
     work.end()
-    to_across.wait_send()
-    forward.wait()
+    for copy in to_across:
+        copy.wait_send()
+    for copy in forwards:
+        copy.wait()
 
 
 def near_reduce(acc, jac, devices):
@@ -379,12 +408,12 @@
         name="near_reduce",
         out_shape=(
             jax.ShapeDtypeStruct((rows, columns), jnp.float32),
-            jax.ShapeDtypeStruct((2, slots - slots // 2, depth, width), jnp.float32),
+            jax.ShapeDtypeStruct((2, slots - slots // 4, depth, width), jnp.float32),
         ),
         in_specs=[ANY, ANY],
         out_specs=(VMEM, ANY),
         scratch_shapes=reduction_scratch(bits, rows, width, columns // width)
-        + [pltpu.SemaphoreType.DMA((2,)), pltpu.SemaphoreType.DMA((2,))],
+        + [pltpu.SemaphoreType.DMA((2 * CHUNKS,))] * 2,
         compiler_params=pltpu.CompilerParams(
             collective_id=1, has_side_effects=True, vmem_limit_bytes=VMEM_LIMIT
         ),

time: 97.4 us -> 92.2 us (0.947)
  Pallas kernels: 94.7 us -> 88.9 us
    pallas_call x1, Pallas kernels: 30.6 us -> 24.7 us  [exchange(): pl.pallas_call(exchange_kernel, name='camera_exchange', out_shape=(jax.Sh...]
    pallas_call x1, Pallas kernels: 26.3 us -> 23.1 us  [near_reduce(): pl.pallas_call(functools.partial(near_reduce_kernel, bits, width), name='...]
    pallas_call x1, Pallas kernels: 3.9 us -> 6.45 us  [near_sum(): pl.pallas_call(near_kernel, name='near_sum', out_shape=(jax.ShapeDtypeStr...]
    pallas_call x1, Pallas kernels: 3.25 us -> 4.9 us  [far_sum(): pl.pallas_call(far_kernel, name='far_sum', out_shape=jax.ShapeDtypeStruct...]
where the time goes in v3:
time: 92.2 us; the launch traced here: 90.8 us
  Pallas kernels  88.9 us (96%)
  local copies, waits for them, and re-layouts  1.87 us (2%)
    pallas_call x1, Pallas kernels, far_reduce(): pl.pallas_call(functools.partial(far_reduce_kernel, bits, width), name='f...  29.8 us
    pallas_call x1, Pallas kernels, exchange(): pl.pallas_call(exchange_kernel, name='camera_exchange', out_shape=(jax.Sh...  24.7 us
    pallas_call x1, Pallas kernels, near_reduce(): pl.pallas_call(functools.partial(near_reduce_kernel, bits, width), name='...  23.1 us
    pallas_call x1, Pallas kernels, near_sum(): pl.pallas_call(near_kernel, name='near_sum', out_shape=(jax.ShapeDtypeStr...  6.45 us
    pallas_call x1, Pallas kernels, far_sum(): pl.pallas_call(far_kernel, name='far_sum', out_shape=jax.ShapeDtypeStruct...  4.9 us
    unnamed x1, local copies, waits for them, and re-layouts  1.87 us

profile of v3, /device:TPU:0, one launch (start us, length us, event | category | flops | bytes accessed | tf_op | source)
XLA Modules:
  0.0 90.8 jit_solution(17630606490407032582)
XLA Ops:
  0.0 24.7 %camera_exchange.1 = (f32[16,128,128]{2,1,0:T(8,128)}, f32[2,4,128,128]{3,2,1,0:T(8,128)}, f32[16,128,128]{2,1,0:T(8,128)}) custom-call(f32[16,128,128]{2,1,0:T(8,128)} %jac.5, f32[16,3,128,128]{3,2,1,0:T(8,128)} %bitcast.7, f32[3,3,16,128]{3,2,1,0:T(8,128)} %bitcast.10), custom_call_target="tpu_custom_call" | custom-call | tf_op jit(solution)/shard_map/camera_exchange/pallas_call | solution.py:128
  24.7 6.4 %near_sum.1 = (f32[512,384]{1,0:T(8,128)}, f32[16,128,128]{2,1,0:T(8,128)}) custom-call(s32[8]{0:T(128)} %counts.3, s32[4,128]{1,0:T(4,128)} %bitcast.11, f32[16,128,128]{2,1,0:T(8,128)} %jac.5, f32[16,128,128]{2,1,0:T(8,128)} %get-tuple-element.12.near, f32[16,128,128]{2,1,0:T(8,128)} %get-tuple-element.13.coupled), custom_call_target="tpu_custom_call" | custom-call | tf_op jit(solution)/shard_map/near_sum/pallas_call | solution.py:194
  31.1 23.1 %near_reduce.1 = (f32[64,384]{1,0:T(8,128)}, f32[2,12,128,128]{3,2,1,0:T(8,128)}) custom-call(f32[2,2,2,64,384]{4,3,2,1,0:T(8,128)} %bitcast.9, f32[16,128,128]{2,1,0:T(8,128)} %jac.5), custom_call_target="tpu_custom_call" | custom-call | tf_op jit(solution)/shard_map/near_reduce/pallas_call | solution.py:406
  54.2 4.9 %far_sum.1 = f32[512,512]{1,0:T(8,128)} custom-call(s32[8]{0:T(128)} %counts.3, s32[4,128]{1,0:T(4,128)} %bitcast.12, f32[16,128,128]{2,1,0:T(8,128)} %get-tuple-element.14.left, f32[2,4,128,128]{3,2,1,0:T(8,128)} %get-tuple-element.15.early, f32[2,12,128,128]{3,2,1,0:T(8,128)} %get-tuple-element.17.late), custom_call_target="tpu_custom_call" | custom-call | tf_op jit(solution)/shard_map/far_sum/pallas_call | solution.py:244
  59.1 29.8 %far_reduce.1 = f32[64,2048]{1,0:T(8,128)} custom-call(f32[2,2,2,64,512]{4,3,2,1,0:T(8,128)} %bitcast.6, f32[64,384]{1,0:T(8,128)} %get-tuple-element.18.near), custom_call_target="tpu_custom_call" | custom-call | tf_op jit(solution)/shard_map/far_reduce/pallas_call | solution.py:498
  88.9 1.9 %copy.7 = f32[1,64,2048]{2,1,0:T(8,128)} copy(f32[1,64,2048]{2,1,0:T(8,128)} %bitcast.8) | data formatting | bytes 1048576

commit v4 on v3

--- a/solution.py
+++ b/solution.py
@@ -15,8 +15,13 @@
 LANES = 128
 GROUP_TILES = 4
 STRIDE = 4
-CHUNKS = 3
+FAR_STRIDE = 2
+CHUNKS = 2
 VMEM_LIMIT = 56 * 1024 * 1024
+
+
+def early_slots(slots):
+    return 3 * slots // 8
 
 
 def halves(x):
@@ -53,7 +58,7 @@
 
 def exchange_kernel(
     jac, points, inv, near, far, coupled,
-    points_here, outgoing, arrived, mine, across_in,
+    points_here, outgoing, arrived, mine, packed, across_in,
     send_sem, recv_sem, local_sem,
 ):
     camera = lax.axis_index("camera")
@@ -98,6 +103,27 @@
         loads[which].wait()
         lax.fori_loop(0, quarter, body, 0, unroll=2)
 
+    rows = coupled.shape[1]
+    row = lax.broadcasted_iota(jnp.int32, (rows, rows), 0)
+    col = lax.broadcasted_iota(jnp.int32, (rows, rows), 1)
+
+    def pack(q):
+        for i in range(quarter // 2):
+            first, second = mine[q, 2 * i], mine[q, 2 * i + 1]
+            diagonal = jnp.sum(jnp.where(row == col, second, 0.0), axis=0, keepdims=True)
+            packed[q, i, :rows] = jnp.where(row <= col, first, second)
+            packed[q, i, rows:] = jnp.broadcast_to(diagonal, (8, rows))
+
+    def unpack(q, block):
+        for i in range(quarter // 2):
+            both = packed[q, i, :rows] + across_in[q, i, :rows]
+            diagonal = packed[q, i, rows:rows + 1] + across_in[q, i, rows:rows + 1]
+            turned = both.T
+            block[2 * i] = jnp.where(row <= col, both, turned)
+            block[2 * i + 1] = jnp.where(
+                row == col, diagonal, jnp.where(row > col, both, turned)
+            )
+
     sent, crossed, returned = [], [], []
     for q in range(2):
         couple(2 * q, outgoing)
@@ -105,13 +131,14 @@
         couple(2 * q + 1, mine)
         sent[q].wait_recv()
         mine[q] += arrived[q]
-        crossed.append(copy_to(4 + q, mine.at[q], across_in.at[q], across))
+        pack(q)
+        crossed.append(copy_to(4 + q, packed.at[q], across_in.at[q], across))
     to_across.wait_recv()
     forward = copy_to(6, far.at[0], far.at[1], sibling)
     for q in range(2):
         crossed[q].wait_recv()
         block = coupled.at[pl.ds(own + q * quarter, quarter)]
-        block[...] = mine[q] + across_in[q]
+        unpack(q, block)
         returned.append(copy_to(7 + q, block, block, sibling))
     for copy in [to_across, to_sibling] + sent + crossed:
         copy.wait_send()
@@ -125,19 +152,20 @@
     slots, rows, width = jac.shape
     quarter = slots // 4
     block = pltpu.VMEM((2, quarter, rows, rows), jnp.float32)
+    triangles = pltpu.VMEM((2, quarter // 2, rows + 8, rows), jnp.float32)
     return pl.pallas_call(
         exchange_kernel,
         name="camera_exchange",
         out_shape=(
             jax.ShapeDtypeStruct((slots, rows, width), jnp.float32),
-            jax.ShapeDtypeStruct((2, quarter, rows, width), jnp.float32),
+            jax.ShapeDtypeStruct((2, early_slots(slots), rows, width), jnp.float32),
             jax.ShapeDtypeStruct((slots, rows, rows), jnp.float32),
         ),
         in_specs=[ANY, ANY, VMEM],
         out_specs=(ANY, ANY, VMEM),
         scratch_shapes=[
             pltpu.VMEM((4, quarter) + points.shape[1:], jnp.float32),
-            block, block, block, block,
+            block, block, block, triangles, triangles,
             pltpu.SemaphoreType.DMA((9,)),
             pltpu.SemaphoreType.DMA((9,)),
             pltpu.SemaphoreType.DMA((4,)),
@@ -227,16 +255,16 @@
                 add_pair(tiles, acc, slot, camera, r, column, width, cut)
 
         def body(step, carry):
-            blocks = [one(STRIDE * step + i) for i in range(STRIDE)]
-            for i in range(STRIDE):
-                add(STRIDE * step + i, blocks[i])
+            blocks = [one(FAR_STRIDE * step + i) for i in range(FAR_STRIDE)]
+            for i in range(FAR_STRIDE):
+                add(FAR_STRIDE * step + i, blocks[i])
             return carry
 
         lax.fori_loop(0, steps, body, 0)
 
-    steps = (live + STRIDE - 1) // STRIDE
-    part(early, 0, jnp.minimum(steps, first // STRIDE))
-    part(late, first, jnp.maximum(steps - first // STRIDE, 0))
+    steps = (live + FAR_STRIDE - 1) // FAR_STRIDE
+    part(early, 0, jnp.minimum(steps, first // FAR_STRIDE))
+    part(late, first, jnp.maximum(steps - first // FAR_STRIDE, 0))
 
 
 def far_sum(counts, tiles, left, early, late):
@@ -408,7 +436,7 @@
         name="near_reduce",
         out_shape=(
             jax.ShapeDtypeStruct((rows, columns), jnp.float32),
-            jax.ShapeDtypeStruct((2, slots - slots // 4, depth, width), jnp.float32),
+            jax.ShapeDtypeStruct((2, slots - early_slots(slots), depth, width), jnp.float32),
         ),
         in_specs=[ANY, ANY],
         out_specs=(VMEM, ANY),

time: 92.2 us -> 87.7 us (0.951)
  Pallas kernels: 88.9 us -> 84.4 us
    pallas_call x1, Pallas kernels: 24.7 us -> 22.3 us  [exchange(): pl.pallas_call(exchange_kernel, name='camera_exchange', out_shape=(jax.Sh...]
    pallas_call x1, Pallas kernels: 6.45 us -> 4.06 us  [near_sum(): pl.pallas_call(near_kernel, name='near_sum', out_shape=(jax.ShapeDtypeStr...]
    pallas_call x1, Pallas kernels: 4.9 us -> 3.29 us  [far_sum(): pl.pallas_call(far_kernel, name='far_sum', out_shape=jax.ShapeDtypeStruct...]
    pallas_call x1, Pallas kernels: 29.8 us -> 30.9 us  [far_reduce(): pl.pallas_call(functools.partial(far_reduce_kernel, bits, width), name='f...]
where the time goes in v4:
time: 87.7 us; the launch traced here: 86.3 us
  Pallas kernels  84.4 us (96%)
  local copies, waits for them, and re-layouts  1.87 us (2%)
    pallas_call x1, Pallas kernels, far_reduce(): pl.pallas_call(functools.partial(far_reduce_kernel, bits, width), name='f...  30.9 us
    pallas_call x1, Pallas kernels, near_reduce(): pl.pallas_call(functools.partial(near_reduce_kernel, bits, width), name='...  23.9 us
    pallas_call x1, Pallas kernels, exchange(): pl.pallas_call(exchange_kernel, name='camera_exchange', out_shape=(jax.Sh...  22.3 us
    pallas_call x1, Pallas kernels, near_sum(): pl.pallas_call(near_kernel, name='near_sum', out_shape=(jax.ShapeDtypeStr...  4.06 us
    pallas_call x1, Pallas kernels, far_sum(): pl.pallas_call(far_kernel, name='far_sum', out_shape=jax.ShapeDtypeStruct...  3.29 us
    unnamed x1, local copies, waits for them, and re-layouts  1.87 us

profile of v4, /device:TPU:0, one launch (start us, length us, event | category | flops | bytes accessed | tf_op | source)
XLA Modules:
  0.0 86.3 jit_solution(1015424926465360006)
XLA Ops:
  0.0 22.3 %camera_exchange.1 = (f32[16,128,128]{2,1,0:T(8,128)}, f32[2,6,128,128]{3,2,1,0:T(8,128)}, f32[16,128,128]{2,1,0:T(8,128)}) custom-call(f32[16,128,128]{2,1,0:T(8,128)} %jac.5, f32[16,3,128,128]{3,2,1,0:T(8,128)} %bitcast.7, f32[3,3,16,128]{3,2,1,0:T(8,128)} %bitcast.10), custom_call_target="tpu_custom_call" | custom-call | tf_op jit(solution)/shard_map/camera_exchange/pallas_call | solution.py:156
  22.3 4.1 %near_sum.1 = (f32[512,384]{1,0:T(8,128)}, f32[16,128,128]{2,1,0:T(8,128)}) custom-call(s32[8]{0:T(128)} %counts.3, s32[4,128]{1,0:T(4,128)} %bitcast.11, f32[16,128,128]{2,1,0:T(8,128)} %jac.5, f32[16,128,128]{2,1,0:T(8,128)} %get-tuple-element.12.near, f32[16,128,128]{2,1,0:T(8,128)} %get-tuple-element.13.coupled), custom_call_target="tpu_custom_call" | custom-call | tf_op jit(solution)/shard_map/near_sum/pallas_call | solution.py:222
  26.3 23.9 %near_reduce.1 = (f32[64,384]{1,0:T(8,128)}, f32[2,10,128,128]{3,2,1,0:T(8,128)}) custom-call(f32[2,2,2,64,384]{4,3,2,1,0:T(8,128)} %bitcast.9, f32[16,128,128]{2,1,0:T(8,128)} %jac.5), custom_call_target="tpu_custom_call" | custom-call | tf_op jit(solution)/shard_map/near_reduce/pallas_call | solution.py:434
  50.3 3.3 %far_sum.1 = f32[512,512]{1,0:T(8,128)} custom-call(s32[8]{0:T(128)} %counts.3, s32[4,128]{1,0:T(4,128)} %bitcast.12, f32[16,128,128]{2,1,0:T(8,128)} %get-tuple-element.14.left, f32[2,6,128,128]{3,2,1,0:T(8,128)} %get-tuple-element.15.early, f32[2,10,128,128]{3,2,1,0:T(8,128)} %get-tuple-element.17.late), custom_call_target="tpu_custom_call" | custom-call | tf_op jit(solution)/shard_map/far_sum/pallas_call | solution.py:272
  53.6 30.9 %far_reduce.1 = f32[64,2048]{1,0:T(8,128)} custom-call(f32[2,2,2,64,512]{4,3,2,1,0:T(8,128)} %bitcast.6, f32[64,384]{1,0:T(8,128)} %get-tuple-element.18.near), custom_call_target="tpu_custom_call" | custom-call | tf_op jit(solution)/shard_map/far_reduce/pallas_call | solution.py:526
  84.4 1.9 %copy.7 = f32[1,64,2048]{2,1,0:T(8,128)} copy(f32[1,64,2048]{2,1,0:T(8,128)} %bitcast.8) | data formatting | bytes 1048576

commit v5 on v4

--- a/solution.py
+++ b/solution.py
@@ -373,9 +373,7 @@
     straight = tuple(range(bits))
     swapped = (1, 0) + straight[2:]
     far_first = (bits - 1,) + straight[:-1]
-    if parts % 2:
-        return [(straight, swapped, far_first)[part % 3] for part in range(parts)]
-    return [(straight, swapped)[part % 2] for part in range(parts)]
+    return [(straight, swapped, far_first)[part % 3] for part in range(parts)]
 
 
 def near_reduce_kernel(bits, width, given, jac, out, far, acc, *scratch):

time: 87.7 us -> 86 us (0.981)
  Pallas kernels: 84.4 us -> 83.1 us
    pallas_call x1, Pallas kernels: 30.9 us -> 29 us  [far_reduce(): pl.pallas_call(functools.partial(far_reduce_kernel, bits, width), name='f...]
    pallas_call x1, Pallas kernels: 23.9 us -> 23 us  [near_reduce(): pl.pallas_call(functools.partial(near_reduce_kernel, bits, width), name='...]
where the time goes in v5:
time: 86 us; the launch traced here: 85 us
  Pallas kernels  83.1 us (97%)
  local copies, waits for them, and re-layouts  1.87 us (2%)
    pallas_call x1, Pallas kernels, far_reduce(): pl.pallas_call(functools.partial(far_reduce_kernel, bits, width), name='f...  29 us
    pallas_call x1, Pallas kernels, near_reduce(): pl.pallas_call(functools.partial(near_reduce_kernel, bits, width), name='...  23 us
    pallas_call x1, Pallas kernels, exchange(): pl.pallas_call(exchange_kernel, name='camera_exchange', out_shape=(jax.Sh...  22.3 us
    pallas_call x1, Pallas kernels, near_sum(): pl.pallas_call(near_kernel, name='near_sum', out_shape=(jax.ShapeDtypeStr...  4.9 us
    pallas_call x1, Pallas kernels, far_sum(): pl.pallas_call(far_kernel, name='far_sum', out_shape=jax.ShapeDtypeStruct...  3.92 us
    unnamed x1, local copies, waits for them, and re-layouts  1.87 us

profile of v5, /device:TPU:0, one launch (start us, length us, event | category | flops | bytes accessed | tf_op | source)
XLA Modules:
  0.0 85.0 jit_solution(17049137142444854308)
XLA Ops:
  0.0 22.3 %camera_exchange.1 = (f32[16,128,128]{2,1,0:T(8,128)}, f32[2,6,128,128]{3,2,1,0:T(8,128)}, f32[16,128,128]{2,1,0:T(8,128)}) custom-call(f32[16,128,128]{2,1,0:T(8,128)} %jac.5, f32[16,3,128,128]{3,2,1,0:T(8,128)} %bitcast.7, f32[3,3,16,128]{3,2,1,0:T(8,128)} %bitcast.10), custom_call_target="tpu_custom_call" | custom-call | tf_op jit(solution)/shard_map/camera_exchange/pallas_call | solution.py:156
  22.3 4.9 %near_sum.1 = (f32[512,384]{1,0:T(8,128)}, f32[16,128,128]{2,1,0:T(8,128)}) custom-call(s32[8]{0:T(128)} %counts.3, s32[4,128]{1,0:T(4,128)} %bitcast.11, f32[16,128,128]{2,1,0:T(8,128)} %jac.5, f32[16,128,128]{2,1,0:T(8,128)} %get-tuple-element.12.near, f32[16,128,128]{2,1,0:T(8,128)} %get-tuple-element.13.coupled), custom_call_target="tpu_custom_call" | custom-call | tf_op jit(solution)/shard_map/near_sum/pallas_call | solution.py:222
  27.2 23.0 %near_reduce.1 = (f32[64,384]{1,0:T(8,128)}, f32[2,10,128,128]{3,2,1,0:T(8,128)}) custom-call(f32[2,2,2,64,384]{4,3,2,1,0:T(8,128)} %bitcast.9, f32[16,128,128]{2,1,0:T(8,128)} %jac.5), custom_call_target="tpu_custom_call" | custom-call | tf_op jit(solution)/shard_map/near_reduce/pallas_call | solution.py:432
  50.2 3.9 %far_sum.1 = f32[512,512]{1,0:T(8,128)} custom-call(s32[8]{0:T(128)} %counts.3, s32[4,128]{1,0:T(4,128)} %bitcast.12, f32[16,128,128]{2,1,0:T(8,128)} %get-tuple-element.14.left, f32[2,6,128,128]{3,2,1,0:T(8,128)} %get-tuple-element.15.early, f32[2,10,128,128]{3,2,1,0:T(8,128)} %get-tuple-element.17.late), custom_call_target="tpu_custom_call" | custom-call | tf_op jit(solution)/shard_map/far_sum/pallas_call | solution.py:272
  54.1 29.0 %far_reduce.1 = f32[64,2048]{1,0:T(8,128)} custom-call(f32[2,2,2,64,512]{4,3,2,1,0:T(8,128)} %bitcast.6, f32[64,384]{1,0:T(8,128)} %get-tuple-element.18.near), custom_call_target="tpu_custom_call" | custom-call | tf_op jit(solution)/shard_map/far_reduce/pallas_call | solution.py:524
  83.1 1.9 %copy.7 = f32[1,64,2048]{2,1,0:T(8,128)} copy(f32[1,64,2048]{2,1,0:T(8,128)} %bitcast.8) | data formatting | bytes 1048576
